TPU v7x, 128 devices: a whole 4x4x4 slice. The times are simulated.
128 devices in a mesh: freq: 8 (over x, y_lo), mat: 16 (over z, y_hi, core).
Axes of the slice: x: 4, y: 4 (y_hi: 2, y_lo: 2; y = y_hi * 2 + y_lo), z: 4, core: 2. Of those that a mesh axis runs over, the one named last changes fastest.
Arguments:
- traces: bfloat16 [2048, 64, 4096], P('freq', None, 'mat'), may hold values from -6 to 6
- reflection: bfloat16 [16, 2, 4096, 4096], P('freq', None, 'mat'), may hold values from -0.0625 to 0.0625
- onset: int32 [64, 4096], P(None, 'mat'), may hold values from 512 to 2047
Outputs:
- windowed: bfloat16 [2048, 64, 4096], P('freq', None, 'mat')
Inputs may be any that keep to these rules, and one draw needn't show every extreme that they name: onset sample of the direct arrival for each focal point and receiver.
All inputs are finite; a program needn't handle non-finite values.
Results may differ from a plain program's by a relative error of at most 0.0069.
Values may be sent and summed in bfloat16 or wider, within the bound.
A program may use at most 128 MiB of HBM per device.

v0:
```python
import math
import jax
import jax.numpy as jnp
from jax import lax
from jax.sharding import PartitionSpec as P


def forward_table(
    base_band, first_band, band_count, earliest_sample_time, sample_time_count, sampling_interval
):
    angular_freq_list = base_band + first_band + jnp.arange(band_count, dtype=jnp.int32)
    sample_moments = earliest_sample_time + jnp.arange(sample_time_count, dtype=jnp.int32)
    phase_angles = (
        angular_freq_list[:, None] * sample_moments[None, :] % sampling_interval
    ).astype(jnp.float32) * (2.0 * math.pi / sampling_interval)
    factor = 1.0 / math.sqrt(sampling_interval)
    table = jnp.stack([jnp.cos(phase_angles) * factor, -jnp.sin(phase_angles) * factor], axis=1)
    return table.reshape(2 * band_count, sample_time_count).astype(jnp.bfloat16)


def inverse_table(
    base_band,
    first_band,
    band_count,
    earliest_sample_time,
    sample_time_count,
    sampling_interval,
    bands_total,
):
    angular_freq_list = base_band + first_band + jnp.arange(band_count, dtype=jnp.int32)
    sample_moments = earliest_sample_time + jnp.arange(sample_time_count, dtype=jnp.int32)
    phase_angles = (
        sample_moments[:, None] * angular_freq_list[None, :] % sampling_interval
    ).astype(jnp.float32) * (2.0 * math.pi / sampling_interval)
    factor = 1.0 / math.sqrt(bands_total)
    table = jnp.stack([jnp.cos(phase_angles) * factor, -jnp.sin(phase_angles) * factor], axis=2)
    return table.reshape(sample_time_count, 2 * band_count).astype(jnp.bfloat16)


def accumulate(reflection, panels):
    return jnp.einsum("kcpw,kdrw->kcpdr", panels, reflection, preferred_element_type=jnp.float32)


def on_device(traces, reflection, onset):
    temporal_rows, focal_count, recv_rows = traces.shape
    freq_devices = lax.axis_size("freq")
    sampling_interval = temporal_rows * freq_devices
    per_device = reflection.shape[0]
    bands_total = per_device * freq_devices
    base_band = sampling_interval // 16
    earliest_sample_time = lax.axis_index("freq") * temporal_rows
    earliest = lax.axis_index("freq") * temporal_rows
    forward = forward_table(base_band, 0, bands_total, earliest, temporal_rows, sampling_interval)
    partial = jnp.dot(
        forward, traces.reshape(temporal_rows, -1), preferred_element_type=jnp.float32
    )
    partial = partial.astype(jnp.bfloat16).reshape(
        freq_devices, per_device, 2, focal_count, recv_rows
    )
    parts = lax.all_to_all(partial, "freq", split_axis=0, concat_axis=0, tiled=True)
    spectra = jnp.sum(parts.astype(jnp.float32), axis=0).astype(jnp.bfloat16)
    products = accumulate(reflection, lax.all_gather(spectra, "mat", axis=3, tiled=True))
    real_part = products[:, 0, :, 0] - products[:, 1, :, 1]
    imag_part = products[:, 1, :, 0] + products[:, 0, :, 1]
    response = jnp.stack([real_part, imag_part], axis=1).astype(jnp.bfloat16)
    pieces = lax.all_gather(response, "freq", axis=0, tiled=True)
    piece_bands = pieces.shape[0]
    table = inverse_table(
        base_band,
        jnp.int32(0),
        piece_bands,
        earliest_sample_time,
        temporal_rows,
        sampling_interval,
        bands_total,
    )
    wavelet_trace = jnp.dot(
        table, pieces.reshape(2 * piece_bands, -1), preferred_element_type=jnp.float32
    )
    wavelet_trace = wavelet_trace.reshape(temporal_rows, focal_count, recv_rows)
    sample_moments = earliest_sample_time + jnp.arange(temporal_rows, dtype=jnp.int32)
    return jnp.where(sample_moments[:, None, None] < onset[None], wavelet_trace, 0.0).astype(
        jnp.bfloat16
    )


def solution(mesh):
    placed = (P("freq", None, "mat"), P("freq", None, "mat", None), P(None, "mat"))
    return jax.shard_map(
        on_device, mesh=mesh, in_specs=placed, out_specs=P("freq", None, "mat"), check_vma=False
    )
```

profile of v0, /device:TPU:0, one launch (start us, length us, event | category | flops | bytes accessed | tf_op | source)
XLA Modules:
  0.0 166.1 jit_solution(9028758283541389684)
XLA Ops:
  6.5 0.0 all-gather.3.cloned.1.call-start
  6.5 0.2 multiply_convert_fusion.1
  6.8 15.4 %copy.29 = bf16[32,8,64,256]{3,1,2,0:T(8,128)(2,1)} copy(bf16[32,8,64,256]{3,2,1,0:T(8,128)(2,1)} %bitcast.51) | data formatting | bytes 16777216
  22.2 4.9 %convolution_convert_fusion = bf16[32,16384]{1,0:T(8,128)(2,1)S(1)} fusion(bf16[32,256]{1,0:T(8,128)(2,1)S(1)} %convert_element_type.60, bf16[256,16384]{1,0:T(8,128)(2,1)} %bitcast.50), kind=kOutput, calls=%fused_computation | convolution fusion | flops 268959744 | bytes 9453568 | tf_op jit(solution)/shard_map/dot_general | solution.py:54
  27.1 0.2 copy.30
  27.3 0.0 copy-start
  27.4 20.7 %all_to_all.5 = bf16[8,2,2,64,256]{4,3,2,1,0:T(8,128)(2,1)S(1)} all-to-all(bf16[8,2,2,64,256]{4,3,2,1,0:T(8,128)(2,1)S(1)} %bitcast.53), channel_id=1, replica_groups=mesh['freq'=8,'mat'=16] {'freq'}, dimensions={0} | all-to-all | bytes 2097152 | tf_op jit(solution)/shard_map/all_to_all | solution.py:60
  48.0 0.8 reduce_sum.12
  48.8 0.0 all-gather.3.cloned.1.call-update
  48.9 0.2 all-gather.5.cloned.1.call-start
  49.1 47.8 %all-gather.3.cloned.1.call-done = bf16[2,2,64,4096]{3,2,1,0:T(8,128)(2,1)} async-done(((bf16[2,2,64,256]{3,2,1,0:T(8,128)(2,1)}), bf16[2,2,64,4096]{3,2,1,0:T(8,128)(2,1)}) %all-gather.3.cloned.1.call-update) | async-done | bytes 2097168 | tf_op jit(solution)/shard_map/all_gather | solution.py:62
  96.9 6.9 %fusion = f32[2,2,64,2,256]{4,2,3,1,0:T(8,128)S(1)} fusion(bf16[2,2,256,4096]{3,2,1,0:T(8,128)(2,1)} %param.4, bf16[2,2,64,4096]{3,2,1,0:T(8,128)(2,1)} %all-gather.3.cloned.1.call-done), kind=kOutput, calls=%fused_computation.2 | convolution fusion | flops 1073741824 | bytes 11010048 | tf_op jit(solution)/shard_map/kcpw,kdrw->kcpdr/dot_general | solution.py:41
  103.9 0.7 pad_maximum_fusion
  104.5 0.0 all-gather.5.cloned.1.call-update
  104.6 0.2 multiply_convert_fusion.3
  104.8 37.0 %all-gather.5.cloned.1.call-done = bf16[16,2,64,256]{3,2,0,1:T(8,128)(2,1)} async-done(((bf16[2,2,64,256]{3,2,0,1:T(8,128)(2,1)}), bf16[16,2,64,256]{3,2,0,1:T(8,128)(2,1)}) %all-gather.5.cloned.1.call-update) | async-done | bytes 1048592 | tf_op jit(solution)/shard_map/all_gather | solution.py:66
  141.8 1.3 copy.21
  143.0 0.0 copy-done
  143.1 4.7 %select_convert_fusion = bf16[256,64,256]{2,0,1:T(8,128)(2,1)} fusion(bf16[256,32,1]{0,1,2:T(8,128)(2,1)S(1)} %reshape.357, s32[64,256]{1,0:T(8,128)S(1)} %copy-done, s32[256]{0:T(256)S(1)} %iota_add_fusion, bf16[4,8,64,256]{3,2,1,0:T(8,128)(2,1)S(1)} %bitcast.54), kind=kOutput, calls=%fused_computation.1 | convolution fusion | flops 281018368 | bytes 9520128 | tf_op jit(solution)/shard_map/dot_general | solution.py:77
  147.7 11.5 %copy.23 = bf16[256,64,256]{2,1,0:T(8,128)(2,1)} copy(bf16[256,64,256]{2,0,1:T(8,128)(2,1)} %select_convert_fusion) | data formatting | bytes 16777216 | tf_op jit(solution)/shard_map/convert_element_type | solution.py:82
  (10 shorter events, 0.1 us)
Async XLA Ops:
  6.5 90.3 %all-gather.3.cloned.1.call-start = ((), (), s32[]{:S(2)}) async-start(), calls=%async_computation.1 | async-start | bytes 2228224 | tf_op jit(solution)/shard_map/all_gather | solution.py:62
  27.3 115.7 %copy-start = (s32[64,256]{1,0:T(8,128)S(1)}, s32[64,256]{1,0:T(8,128)}, u32[]{:S(2)}) copy-start(s32[64,256]{1,0:T(8,128)} %param.5) | copy-start | bytes 196612
  48.9 92.9 %all-gather.5.cloned.1.call-start = ((), (), s32[]{:S(2)}) async-start(), calls=%async_computation.2 | async-start | bytes 1179648 | tf_op jit(solution)/shard_map/all_gather | solution.py:66
Sparse Core Ops, SparseCore 0:
  49.0 47.8 all-gather.2
  104.7 37.0 all-gather.4
where the time goes:
time: 166 us
  waiting for transfers between devices  84.8 us (51%)
  local copies, waits for them, and re-layouts  28.6 us (17%)
  blocking collectives  20.7 us (12%)
  matrix products  16.5 us (10%)
  between operations  13.5 us (8%)
  other arithmetic  1.84 us (1%)
    all_gather x1, waiting for transfers between devices, on_device(): lax.all_gather(spectra, 'mat', axis=3, tiled=True)  47.8 us
    all_gather x1, waiting for transfers between devices, on_device(): pieces = lax.all_gather(response, 'freq', axis=0, tiled=True)  37 us
    all_to_all x1, blocking collectives, on_device(): lax.all_to_all(partial, 'freq', split_axis=0, concat_axis=0, tiled=True)  20.7 us
    unnamed x4, local copies, waits for them, and re-layouts  15.7 us
    convert_element_type x1, local copies, waits for them, and re-layouts, on_device(): jnp.where(sample_moments[:, None, None] < onset[None], wavelet_trace, 0.0)  11.5 us
    dot_general x1, matrix products, accumulate(): jnp.einsum('kcpw,kdrw->kcpdr', panels, reflection, preferred_element_type...  6.94 us
    dot_general x1, matrix products, on_device(): jnp.dot(forward, traces.reshape(temporal_rows, -1), preferred_element_typ...  4.92 us
    dot_general x1, matrix products, on_device(): jnp.dot(table, pieces.reshape(2 * piece_bands, -1), preferred_element_typ...  4.66 us
  transfers between devices with their start and end apart: 2, of which 2 were waited for; matrix products, arithmetic and copies ran while one was open for 0% of the time, Pallas kernels for 0%

commit v1 on v0

--- a/solution.py
+++ b/solution.py
@@ -3,6 +3,7 @@
 import jax.numpy as jnp
 from jax import lax
 from jax.sharding import PartitionSpec as P
+from jax.lax import all_to_all, psum
 
 
 def forward_table(
@@ -59,7 +60,19 @@
     )
     parts = lax.all_to_all(partial, "freq", split_axis=0, concat_axis=0, tiled=True)
     spectra = jnp.sum(parts.astype(jnp.float32), axis=0).astype(jnp.bfloat16)
-    products = accumulate(reflection, lax.all_gather(spectra, "mat", axis=3, tiled=True))
+
+    def unite_sections_on(a0, mesh_ax):
+        return jnp.concatenate(
+            all_to_all(
+                jnp.stack(psum(1, axis_name=mesh_ax) * [a0], axis=0),
+                axis_name=mesh_ax,
+                split_axis=0,
+                concat_axis=0,
+            ),
+            axis=3,
+        )
+
+    products = accumulate(reflection, unite_sections_on(spectra, "mat"))
     real_part = products[:, 0, :, 0] - products[:, 1, :, 1]
     imag_part = products[:, 1, :, 0] + products[:, 0, :, 1]
     response = jnp.stack([real_part, imag_part], axis=1).astype(jnp.bfloat16)

time: 166 us -> 155 us (0.934)
  waiting for transfers between devices: 84.8 us -> 34.2 us
  blocking collectives: 20.7 us -> 57.3 us
  local copies, waits for them, and re-layouts: 28.6 us -> 32.4 us
    all_gather x1 -> x0, waiting for transfers between devices: 47.8 us -> none  [on_device(): lax.all_gather(spectra, 'mat', axis=3, tiled=True)]
    all_to_all x0 -> x1, blocking collectives: none -> 36.8 us  [unite_sections_on(): all_to_all(jnp.stack(psum(1, axis_name=mesh_ax) * [a0], axis=0), axis_nam...]
    reshape x0 -> x2, local copies, waits for them, and re-layouts: none -> 3.55 us  [unite_sections_on(): jnp.concatenate(all_to_all(jnp.stack(psum(1, axis_name=mesh_ax) * [a0], a...]
    all_gather x1, waiting for transfers between devices: 37 us -> 34.2 us  [on_device(): pieces = lax.all_gather(response, 'freq', axis=0, tiled=True)]
  transfers between devices with their start and end apart: 2 -> 1, of which waited for: 2 -> 1; matrix products, arithmetic and copies ran while one was open for 0% -> 0% of each run, Pallas kernels for 0% -> 0%
where the time goes in v1:
time: 155 us
  blocking collectives  57.3 us (37%)
  waiting for transfers between devices  34.2 us (22%)
  local copies, waits for them, and re-layouts  32.4 us (21%)
  matrix products  16.5 us (11%)
  between operations  13.5 us (9%)
    all_to_all x1, blocking collectives, unite_sections_on(): all_to_all(jnp.stack(psum(1, axis_name=mesh_ax) * [a0], axis=0), axis_nam...  36.8 us
    all_gather x1, waiting for transfers between devices, on_device(): pieces = lax.all_gather(response, 'freq', axis=0, tiled=True)  34.2 us
    all_to_all x1, blocking collectives, on_device(): lax.all_to_all(partial, 'freq', split_axis=0, concat_axis=0, tiled=True)  20.5 us
    unnamed x4, local copies, waits for them, and re-layouts  15.7 us
    convert_element_type x1, local copies, waits for them, and re-layouts, on_device(): jnp.where(sample_moments[:, None, None] < onset[None], wavelet_trace, 0.0)  11.5 us
    dot_general x1, matrix products, accumulate(): jnp.einsum('kcpw,kdrw->kcpdr', panels, reflection, preferred_element_type...  6.94 us
    dot_general x1, matrix products, on_device(): jnp.dot(forward, traces.reshape(temporal_rows, -1), preferred_element_typ...  4.92 us
    dot_general x1, matrix products, on_device(): jnp.dot(table, pieces.reshape(2 * piece_bands, -1), preferred_element_typ...  4.66 us
  transfers between devices with their start and end apart: 1, of which 1 were waited for; matrix products, arithmetic and copies ran while one was open for 0% of the time, Pallas kernels for 0%

profile of v1, /device:TPU:0, one launch (start us, length us, event | category | flops | bytes accessed | tf_op | source)
XLA Modules:
  0.0 155.1 jit_solution(15277624855126942181)
XLA Ops:
  6.5 0.0 all-gather.2.cloned.1.call-start
  6.5 0.2 multiply_convert_fusion.1
  6.8 15.4 %copy.37 = bf16[32,8,64,256]{3,1,2,0:T(8,128)(2,1)} copy(bf16[32,8,64,256]{3,2,1,0:T(8,128)(2,1)} %bitcast.52) | data formatting | bytes 16777216
  22.2 4.9 %convolution_convert_fusion = bf16[32,16384]{1,0:T(8,128)(2,1)S(1)} fusion(bf16[32,256]{1,0:T(8,128)(2,1)S(1)} %convert_element_type.60, bf16[256,16384]{1,0:T(8,128)(2,1)} %bitcast.51), kind=kOutput, calls=%fused_computation | convolution fusion | flops 268959744 | bytes 9453568 | tf_op jit(solution)/shard_map/dot_general | solution.py:55
  27.1 0.2 copy.38
  27.3 20.5 %all_to_all.10 = bf16[8,2,2,64,256]{4,3,2,1,0:T(8,128)(2,1)S(1)} all-to-all(bf16[8,2,2,64,256]{4,3,2,1,0:T(8,128)(2,1)S(1)} %bitcast.55), channel_id=1, replica_groups=mesh['freq'=8,'mat'=16] {'freq'}, dimensions={0} | all-to-all | bytes 2097152 | tf_op jit(solution)/shard_map/all_to_all | solution.py:61
  47.9 0.1 reduce_sum.12
  48.0 0.2 stack.13
  48.3 36.8 %all_to_all.11 = bf16[16,2,2,64,256]{4,3,2,1,0:T(8,128)(2,1)S(1)} all-to-all(bf16[16,2,2,64,256]{4,3,2,1,0:T(8,128)(2,1)S(1)} %stack.13), channel_id=1, replica_groups=mesh['freq'=8,'mat'=16] {'mat'}, dimensions={0} | all-to-all | bytes 4194304 | tf_op jit(solution)/shard_map/all_to_all | solution.py:66
  85.1 1.2 copy.26
  86.3 0.0 copy-start
  86.3 2.3 %reshape.365 = bf16[2,2,64,4096,1]{3,2,1,0,4:T(8,128)(2,1)} reshape(bf16[2,2,64,16,256]{4,3,2,1,0:T(8,128)(2,1)S(1)} %copy.26) | data formatting | bytes 4194304 | tf_op jit(solution)/shard_map/reshape | solution.py:65
  88.6 6.9 %fusion = f32[2,2,64,2,256]{4,2,3,1,0:T(8,128)S(1)} fusion(bf16[2,2,256,4096]{3,2,1,0:T(8,128)(2,1)} %param.4, bf16[2,2,64,4096,1]{3,2,1,0,4:T(8,128)(2,1)} %reshape.365), kind=kOutput, calls=%fused_computation.2 | convolution fusion | flops 1073741824 | bytes 11010048 | tf_op jit(solution)/shard_map/kcpw,kdrw->kcpdr/dot_general | solution.py:42
  95.6 0.7 pad_maximum_fusion
  96.3 0.0 all-gather.2.cloned.1.call-update
  96.3 0.2 multiply_convert_fusion.3
  96.5 34.2 %all-gather.2.cloned.1.call-done = bf16[16,2,64,256]{3,2,0,1:T(8,128)(2,1)} async-done(((bf16[2,2,64,256]{3,2,0,1:T(8,128)(2,1)}), bf16[16,2,64,256]{3,2,0,1:T(8,128)(2,1)}) %all-gather.2.cloned.1.call-update) | async-done | bytes 1048592 | tf_op jit(solution)/shard_map/all_gather | solution.py:79
  130.7 1.3 copy.29
  132.0 0.0 copy-done
  132.0 4.7 %select_convert_fusion = bf16[256,64,256]{2,0,1:T(8,128)(2,1)} fusion(bf16[256,32,1]{0,1,2:T(8,128)(2,1)S(1)} %reshape.367, s32[64,256]{1,0:T(8,128)S(1)} %copy-done, s32[256]{0:T(256)S(1)} %iota_add_fusion, bf16[4,8,64,256]{3,2,1,0:T(8,128)(2,1)S(1)} %bitcast.56), kind=kOutput, calls=%fused_computation.1 | convolution fusion | flops 281018368 | bytes 9520128 | tf_op jit(solution)/shard_map/dot_general | solution.py:90
  136.7 11.5 %copy.31 = bf16[256,64,256]{2,1,0:T(8,128)(2,1)} copy(bf16[256,64,256]{2,0,1:T(8,128)(2,1)} %select_convert_fusion) | data formatting | bytes 16777216 | tf_op jit(solution)/shard_map/convert_element_type | solution.py:95
  (10 shorter events, 0.1 us)
Async XLA Ops:
  6.5 124.2 %all-gather.2.cloned.1.call-start = ((), (), s32[]{:S(2)}) async-start(), calls=%async_computation.2 | async-start | bytes 1179648 | tf_op jit(solution)/shard_map/all_gather | solution.py:79
  86.3 45.7 %copy-start = (s32[64,256]{1,0:T(8,128)S(1)}, s32[64,256]{1,0:T(8,128)}, u32[]{:S(2)}) copy-start(s32[64,256]{1,0:T(8,128)} %param.5) | copy-start | bytes 196612
Sparse Core Ops, SparseCore 0:
  96.4 34.2 all-gather.1
